TPU v7x, 128 devices: a whole 4x4x4 slice. The times are simulated.
128 devices in a mesh: dp: 4 (over y_hi, core), fsdp: 32 (over z, y_lo, x).
Axes of the slice: x: 4, y: 4 (y_hi: 2, y_lo: 2; y = y_hi * 2 + y_lo), z: 4, core: 2. Of those that a mesh axis runs over, the one named last changes fastest.
Arguments:
- tokens: bfloat16 [2, 65536, 768], P(None, ('dp', 'fsdp')), may hold values from -6 to 6
- parts: int32 [2, 128, 8], P(None, ('dp', 'fsdp')), may hold values from 1 to 128, 512 in all within a row
- cotangent: bfloat16 [2, 65536, 768], P(None, ('dp', 'fsdp'))
- w_query: bfloat16 [768, 768], P(('dp', 'fsdp')), may hold values from -0.21875 to 0.21875
- w_key: bfloat16 [768, 768], P(('dp', 'fsdp')), may hold values from -0.21875 to 0.21875
- w_value: bfloat16 [768, 768], P(('dp', 'fsdp')), may hold values from -0.21875 to 0.21875
- w_out: bfloat16 [768, 768], P(('dp', 'fsdp')), may hold values from -0.625 to 0.625
- w_up: bfloat16 [768, 3072], P(('dp', 'fsdp')), may hold values from -0.21875 to 0.21875
- w_down: bfloat16 [3072, 768], P(('dp', 'fsdp')), may hold values from -0.109375 to 0.109375
- shared_a: bfloat16 [768, 1024], P(('dp', 'fsdp')), may hold values from -0.21875 to 0.21875
- shared_b: bfloat16 [1024, 768], P(('dp', 'fsdp')), may hold values from -0.1875 to 0.1875
- gain_one: float32 [768], replicated, may hold values from 0.1 to 1.9
- shift_one: float32 [768], replicated, may hold values from -1.5 to 1.5
- gain_two: float32 [768], replicated, may hold values from 0.1 to 1.9
- shift_two: float32 [768], replicated, may hold values from -1.5 to 1.5
- scale_dq: float32 [1024], replicated, may hold values from 0.3 to 1.5
- scale_bq: float32 [768], replicated, may hold values from -2.5 to 2.5
- scale_dv: float32 [1024], replicated, may hold values from 0.3 to 1.5
- scale_bv: float32 [768], replicated, may hold values from -2.5 to 2.5
Outputs:
- output: bfloat16 [2, 65536, 768], P(None, ('dp', 'fsdp'))
- grad_tokens: bfloat16 [2, 65536, 768], P(None, ('dp', 'fsdp'))
- grad_dq: float32 [1024], replicated
- grad_bq: float32 [768], replicated
- grad_dv: float32 [1024], replicated
- grad_bv: float32 [768], replicated
Inputs may be any that keep to these rules, and one draw needn't show every extreme that they name: `parts`: in every packed row the 4 pairs' two sentence lengths fill the row's 512 tokens exactly; entries 2p and 2p+1 are pair p's first and second sentence.
All inputs are finite; a program needn't handle non-finite values.
Results may differ from a plain program's by a relative error of at most 0.014.
Values may be sent and summed in bfloat16 or wider, within the bound.
A program may use at most 256 MiB of HBM per device.

v0:
```python
import math

import jax
import jax.numpy as jnp
from jax import lax
from jax.sharding import PartitionSpec as P

D = 768
HEADS = 12
HEAD_DIM = 64


def product(left, right):
    return jnp.dot(left, right, preferred_element_type=jnp.float32)


def product_t(left, right):
    return lax.dot_general(
        left, right, (((1,), (1,)), ((), ())), preferred_element_type=jnp.float32
    )


def norm_layer(stream, gain_vec, shift_vec):
    average = jnp.mean(stream, axis=-1, keepdims=True)
    centred = stream - average
    variance = jnp.mean(centred * centred, axis=-1, keepdims=True)
    return centred * lax.rsqrt(variance + 1e-05) * gain_vec + shift_vec


def norm_back(stream, gain_vec, shift_vec, incoming):
    pullback = jax.vjp(lambda value: norm_layer(value, gain_vec, shift_vec), stream)[1]
    return pullback(incoming)[0]


def gelu_exact(value):
    return jax.nn.gelu(value, approximate=False)


def pair_mask(lengths, width):
    pair_sizes = lengths[:, 0::2] + lengths[:, 1::2]
    pair_ends = jnp.cumsum(pair_sizes, axis=-1)
    position = jnp.arange(width, dtype=jnp.int32)
    pair_id = jnp.sum((position[None, :, None] >= pair_ends[:, None, :]).astype(jnp.int32), axis=-1)
    return (pair_id[:, :, None] == pair_id[:, None, :])[0]


def forward(row_low, allowed, weights, vectors, norms):
    w_query, w_key, w_value, w_out, w_up, w_down, shared_a, shared_b = weights
    scale_dq, scale_bq, scale_dv, scale_bv = vectors
    gain_one, shift_one, gain_two, shift_two = norms
    length = row_low.shape[0]
    inv_root = 1.0 / math.sqrt(HEAD_DIM)
    stream = row_low.astype(jnp.float32)
    latent = product(row_low, shared_a)
    query_u = (latent * scale_dq).astype(jnp.bfloat16)
    value_u = (latent * scale_dv).astype(jnp.bfloat16)
    query_t = product(query_u, shared_b)
    value_t = product(value_u, shared_b)
    query_rows = (product(row_low, w_query) + scale_bq * query_t).astype(jnp.bfloat16)
    key_rows = product(row_low, w_key).astype(jnp.bfloat16)
    value_rows = (product(row_low, w_value) + scale_bv * value_t).astype(jnp.bfloat16)
    query_heads = query_rows.reshape(length, HEADS, HEAD_DIM)
    key_heads = key_rows.reshape(length, HEADS, HEAD_DIM)
    value_heads = value_rows.reshape(length, HEADS, HEAD_DIM)
    logits = (
        jnp.einsum("lhe,mhe->hlm", query_heads, key_heads, preferred_element_type=jnp.float32)
        * inv_root
    )
    scores = jnp.where(allowed[None], logits, -1e30)
    softmaxed = jax.nn.softmax(scores, axis=-1)
    soft_low = softmaxed.astype(jnp.bfloat16)
    mixed = jnp.einsum("hlm,mhe->lhe", soft_low, value_heads, preferred_element_type=jnp.float32)
    attended = mixed.reshape(length, D).astype(jnp.bfloat16)
    pre_one = stream + product(attended, w_out)
    first = norm_layer(pre_one, gain_one, shift_one)
    upper = product(first.astype(jnp.bfloat16), w_up)
    hidden = gelu_exact(upper).astype(jnp.bfloat16)
    pre_two = first + product(hidden, w_down)
    second = norm_layer(pre_two, gain_two, shift_two)
    saved = (
        latent,
        query_t,
        value_t,
        query_heads,
        key_heads,
        value_heads,
        softmaxed,
        soft_low,
        pre_one,
        upper,
        pre_two,
    )
    return (saved, second.astype(jnp.bfloat16))


def backward(saved, incoming, weights, vectors, norms):
    w_query, w_key, w_value, w_out, w_up, w_down, shared_a, shared_b = weights
    scale_dq, scale_bq, scale_dv, scale_bv = vectors
    gain_one, shift_one, gain_two, shift_two = norms
    (
        latent,
        query_t,
        value_t,
        query_heads,
        key_heads,
        value_heads,
        softmaxed,
        soft_low,
        pre_one,
        upper,
        pre_two,
    ) = saved
    length = incoming.shape[0]
    inv_root = 1.0 / math.sqrt(HEAD_DIM)
    grad_pre_two = norm_back(pre_two, gain_two, shift_two, incoming)
    grad_down = grad_pre_two.astype(jnp.bfloat16)
    grad_hidden = product_t(grad_down, w_down)
    gelu_pull = jax.vjp(gelu_exact, upper)[1]
    grad_upper = gelu_pull(grad_hidden)[0].astype(jnp.bfloat16)
    grad_first = grad_pre_two + product_t(grad_upper, w_up)
    grad_pre_one = norm_back(pre_one, gain_one, shift_one, grad_first)
    grad_proj = grad_pre_one.astype(jnp.bfloat16)
    grad_att = product_t(grad_proj, w_out).astype(jnp.bfloat16)
    grad_heads = grad_att.reshape(length, HEADS, HEAD_DIM)
    grad_soft = jnp.einsum(
        "lhe,mhe->hlm", grad_heads, value_heads, preferred_element_type=jnp.float32
    )
    grad_vals = jnp.einsum("hlm,lhe->mhe", soft_low, grad_heads, preferred_element_type=jnp.float32)
    grad_logits = (
        softmaxed * (grad_soft - jnp.sum(softmaxed * grad_soft, axis=-1, keepdims=True))
    ).astype(jnp.bfloat16)
    grad_query = (
        (
            jnp.einsum("hlm,mhe->lhe", grad_logits, key_heads, preferred_element_type=jnp.float32)
            * inv_root
        )
        .reshape(length, D)
        .astype(jnp.bfloat16)
    )
    grad_keys = (
        (
            jnp.einsum("hlm,lhe->mhe", grad_logits, query_heads, preferred_element_type=jnp.float32)
            * inv_root
        )
        .reshape(length, D)
        .astype(jnp.bfloat16)
    )
    grad_values = grad_vals.reshape(length, D).astype(jnp.bfloat16)
    grad_query_f = grad_query.astype(jnp.float32)
    grad_values_f = grad_values.astype(jnp.float32)
    grad_bq = jnp.sum(grad_query_f * query_t, axis=0)
    grad_bv = jnp.sum(grad_values_f * value_t, axis=0)
    grad_query_u = product_t((grad_query_f * scale_bq).astype(jnp.bfloat16), shared_b)
    grad_value_u = product_t((grad_values_f * scale_bv).astype(jnp.bfloat16), shared_b)
    grad_dq = jnp.sum(grad_query_u * latent, axis=0)
    grad_dv = jnp.sum(grad_value_u * latent, axis=0)
    grad_latent = (grad_query_u * scale_dq + grad_value_u * scale_dv).astype(jnp.bfloat16)
    grad_rows = (
        grad_pre_one
        + product_t(grad_query, w_query)
        + product_t(grad_keys, w_key)
        + product_t(grad_values, w_value)
        + product_t(grad_latent, shared_a)
    )
    return (grad_rows.astype(jnp.bfloat16), (grad_dq, grad_bq, grad_dv, grad_bv))


def shards(
    tokens,
    parts,
    cotangent,
    w_query,
    w_key,
    w_value,
    w_out,
    w_up,
    w_down,
    shared_a,
    shared_b,
    gain_one,
    shift_one,
    gain_two,
    shift_two,
    scale_dq,
    scale_bq,
    scale_dv,
    scale_bv,
):
    vectors = (scale_dq, scale_bq, scale_dv, scale_bv)
    norms = (gain_one, shift_one, gain_two, shift_two)
    running = tuple((jnp.zeros_like(vector) for vector in vectors))
    micro = tokens.shape[0]
    width_row = tokens.shape[1]
    results = []
    grads = []
    for index in range(micro):
        allowed = pair_mask(parts[index], width_row)
        forward_set = (
            lax.all_gather(w_query, ("dp", "fsdp"), axis=0, tiled=True),
            lax.all_gather(w_key, ("dp", "fsdp"), axis=0, tiled=True),
            lax.all_gather(w_value, ("dp", "fsdp"), axis=0, tiled=True),
            lax.all_gather(w_out, ("dp", "fsdp"), axis=0, tiled=True),
            lax.all_gather(w_up, ("dp", "fsdp"), axis=0, tiled=True),
            lax.all_gather(w_down, ("dp", "fsdp"), axis=0, tiled=True),
            lax.all_gather(shared_a, ("dp", "fsdp"), axis=0, tiled=True),
            lax.all_gather(shared_b, ("dp", "fsdp"), axis=0, tiled=True),
        )
        saved, result = forward(tokens[index], allowed, forward_set, vectors, norms)
        backward_set = (
            lax.all_gather(w_query, ("dp", "fsdp"), axis=0, tiled=True),
            lax.all_gather(w_key, ("dp", "fsdp"), axis=0, tiled=True),
            lax.all_gather(w_value, ("dp", "fsdp"), axis=0, tiled=True),
            lax.all_gather(w_out, ("dp", "fsdp"), axis=0, tiled=True),
            lax.all_gather(w_up, ("dp", "fsdp"), axis=0, tiled=True),
            lax.all_gather(w_down, ("dp", "fsdp"), axis=0, tiled=True),
            lax.all_gather(shared_a, ("dp", "fsdp"), axis=0, tiled=True),
            lax.all_gather(shared_b, ("dp", "fsdp"), axis=0, tiled=True),
        )
        grad_rows, terms = backward(
            saved, cotangent[index].astype(jnp.float32), backward_set, vectors, norms
        )
        running = tuple((left + right for left, right in zip(running, terms)))
        results.append(result)
        grads.append(grad_rows)
    summed = lax.psum((running[0], running[1], running[2], running[3]), ("dp", "fsdp"))
    return (jnp.stack(results), jnp.stack(grads), summed[0], summed[1], summed[2], summed[3])


def solution(mesh):
    placed = (
        P(None, ("dp", "fsdp"), None),
        P(None, ("dp", "fsdp"), None),
        P(None, ("dp", "fsdp"), None),
        P(("dp", "fsdp"), None),
        P(("dp", "fsdp"), None),
        P(("dp", "fsdp"), None),
        P(("dp", "fsdp"), None),
        P(("dp", "fsdp"), None),
        P(("dp", "fsdp"), None),
        P(("dp", "fsdp"), None),
        P(("dp", "fsdp"), None),
        P(),
        P(),
        P(),
        P(),
        P(),
        P(),
        P(),
        P(),
    )
    return jax.shard_map(
        shards,
        mesh=mesh,
        in_specs=placed,
        out_specs=(
            P(None, ("dp", "fsdp"), None),
            P(None, ("dp", "fsdp"), None),
            P(),
            P(),
            P(),
            P(),
        ),
        check_vma=False,
    )
```

profile of v0, /device:TPU:1, one launch (start us, length us, event | category | flops | bytes accessed | tf_op | source)
XLA Modules:
  0.0 2673.8 jit_solution(12132049299813476456)
XLA Ops:
  15.4 296.4 %all-gather.25.cloned.1.call-done = bf16[128,6,768]{2,1,0:T(8,128)(2,1)} async-done(((bf16[1,6,768]{2,1,0:T(8,128)(2,1)}), bf16[128,6,768]{2,1,0:T(8,128)(2,1)}) %all-gather.25.cloned.1.call-update) | async-done | bytes 1179664 | tf_op jit(solution)/shard_map/all_gather | solution.py:200
  311.8 2.3 reshape.345
  314.1 2.4 convolution_convert_fusion.2
  319.7 292.5 %all-gather.23.cloned.1.call-done = bf16[128,6,768]{2,1,0:T(8,128)(2,1)} async-done(((bf16[1,6,768]{2,1,0:T(8,128)(2,1)}), bf16[128,6,768]{2,1,0:T(8,128)(2,1)}) %all-gather.23.cloned.1.call-update) | async-done | bytes 1179664 | tf_op jit(solution)/shard_map/all_gather | solution.py:199
  612.2 3.2 reshape.343
  615.4 297.2 %all-gather.19.cloned.1.call-done = bf16[128,6,768]{2,1,0:T(8,128)(2,1)} async-done(((bf16[1,6,768]{2,1,0:T(8,128)(2,1)}), bf16[128,6,768]{2,1,0:T(8,128)(2,1)}) %all-gather.19.cloned.1.call-update) | async-done | bytes 1179664 | tf_op jit(solution)/shard_map/all_gather | solution.py:201
  912.6 2.3 reshape.339
  915.0 297.9 %all-gather.27.cloned.1.call-done = bf16[128,6,768]{2,1,0:T(8,128)(2,1)} async-done(((bf16[1,6,768]{2,1,0:T(8,128)(2,1)}), bf16[128,6,768]{2,1,0:T(8,128)(2,1)}) %all-gather.27.cloned.1.call-update) | async-done | bytes 1179664 | tf_op jit(solution)/shard_map/all_gather | solution.py:202
  1212.9 3.2 reshape.347
  1216.1 299.7 %all-gather.21.cloned.1.call-done = bf16[128,6,1024]{2,1,0:T(8,128)(2,1)} async-done(((bf16[1,6,1024]{2,1,0:T(8,128)(2,1)}), bf16[128,6,1024]{2,1,0:T(8,128)(2,1)}) %all-gather.21.cloned.1.call-update) | async-done | bytes 1572880 | tf_op jit(solution)/shard_map/all_gather | solution.py:205
  1515.9 3.7 reshape.341
  1519.5 2.8 fusion.104
  1522.4 2.4 fusion.109
  1524.7 291.7 %all-gather.15.cloned.1.call-done = bf16[1024,768]{1,0:T(8,128)(2,1)} async-done(((bf16[8,768]{1,0:T(8,128)(2,1)}), bf16[1024,768]{1,0:T(8,128)(2,1)}) %all-gather.15.cloned.1.call-update) | async-done | bytes 1572880 | tf_op jit(solution)/shard_map/all_gather | solution.py:206
  1816.4 2.5 fusion.75
  1821.8 2.4 copy.98
  1824.3 2.7 fusion.74
  1829.8 2.3 copy.97
  1832.1 2.7 fusion.73
  1837.6 2.3 copy.94
  1840.0 2.7 fusion.72
  1847.2 8.3 fusion.158
  1855.5 6.0 fusion.52
  1863.8 7.6 fusion.161
  1871.3 6.2 fusion.58
  1878.9 251.2 %all-gather.29.cloned.1.call-done = bf16[128,6,3072]{2,1,0:T(8,128)(2,1)} async-done(((bf16[1,6,3072]{2,1,0:T(8,128)(2,1)}), bf16[128,6,3072]{2,1,0:T(8,128)(2,1)}) %all-gather.29.cloned.1.call-update) | async-done | bytes 4718608 | tf_op jit(solution)/shard_map/all_gather | solution.py:203
  2130.1 7.8 reshape.349
  2137.9 18.6 fusion.5
  2156.5 284.9 %all-gather.17.cloned.1.call-done = bf16[3072,768]{1,0:T(8,128)(2,1)} async-done(((bf16[24,768]{1,0:T(8,128)(2,1)}), bf16[3072,768]{1,0:T(8,128)(2,1)}) %all-gather.17.cloned.1.call-update) | async-done | bytes 4718608 | tf_op jit(solution)/shard_map/all_gather | solution.py:204
  2441.4 7.9 fusion.163
  2449.3 15.3 fusion.4
  2464.7 2.8 fusion.160
  2470.3 2.8 fusion.154
  2473.1 15.7 multiply_reduce_fusion.7
  2488.8 15.7 multiply_reduce_fusion.6
  2504.6 3.5 fusion.156
  2510.8 7.7 fusion.55
  2518.5 9.0 multiply_reduce_fusion.1
  2527.6 6.9 multiply_convert_fusion.1
  2534.5 2.9 multiply_convert_fusion.12
  2539.7 3.4 fusion.164
  2544.7 6.8 fusion.61
  2551.5 9.2 multiply_reduce_fusion
  2560.7 7.1 multiply_convert_fusion
  2567.9 2.9 multiply_convert_fusion.10
  2572.1 2.0 fusion.166
  2578.5 1.8 fusion.39
  2600.5 66.1 %all-reduce = (f32[1024]{0:T(1024)}, f32[768]{0:T(1024)}, f32[1024]{0:T(1024)}, f32[768]{0:T(1024)}) all-reduce(f32[1024]{0:T(1024)S(1)} %add.190, f32[768]{0:T(1024)S(1)} %add.191, f32[1024]{0:T(1024)S(1)} %add.192, f32[768]{0:T(1024)S(1)} %add.193), channel_id=1, replica_groups=mesh['dp'=4,'fsdp'=32] {'dp','fsdp'}, use_global_device_ids=true, to_apply=%region_28.29 | all-reduce | flops 3584 | bytes 28672 | tf_op jit(solution)/shard_map/psum | solution.py:225
  (262 shorter events, 63.0 us)
Async XLA Ops:
  7.2 304.6 %all-gather.25.cloned.1.call-start = ((), (), s32[]{:S(2)}) async-start(), calls=%async_computation.5 | async-start | bytes 1585152 | tf_op jit(solution)/shard_map/all_gather | solution.py:200
  7.9 604.3 %all-gather.23.cloned.1.call-start = ((), (), s32[]{:S(2)}) async-start(), calls=%async_computation.4 | async-start | bytes 1585152 | tf_op jit(solution)/shard_map/all_gather | solution.py:199
  8.7 904.0 %all-gather.19.cloned.1.call-start = ((), (), s32[]{:S(2)}) async-start(), calls=%async_computation.2 | async-start | bytes 1585152 | tf_op jit(solution)/shard_map/all_gather | solution.py:201
  9.4 1203.5 %all-gather.27.cloned.1.call-start = ((), (), s32[]{:S(2)}) async-start(), calls=%async_computation.6 | async-start | bytes 1585152 | tf_op jit(solution)/shard_map/all_gather | solution.py:202
  10.0 1505.9 %all-gather.21.cloned.1.call-start = ((), (), s32[]{:S(2)}) async-start(), calls=%async_computation.3 | async-start | bytes 2113536 | tf_op jit(solution)/shard_map/all_gather | solution.py:205
  10.5 1805.9 %all-gather.15.cloned.1.call-start = ((), (), s32[]{:S(2)}) async-start(), calls=%async_computation | async-start | bytes 1585152 | tf_op jit(solution)/shard_map/all_gather | solution.py:206
  11.1 2118.9 %all-gather.29.cloned.1.call-start = ((), (), s32[]{:S(2)}) async-start(), calls=%async_computation.7 | async-start | bytes 6340608 | tf_op jit(solution)/shard_map/all_gather | solution.py:203
  11.9 2429.5 %all-gather.17.cloned.1.call-start = ((), (), s32[]{:S(2)}) async-start(), calls=%async_computation.1 | async-start | bytes 4755456 | tf_op jit(solution)/shard_map/all_gather | solution.py:204
  915.0 927.7 %copy-start.9 = (bf16[768,768]{1,0:T(8,128)(2,1)}, bf16[768,768]{1,0:T(8,128)(2,1)S(1)}, u32[]{:S(2)}) copy-start(bf16[768,768]{1,0:T(8,128)(2,1)S(1)} %reshape.339) | copy-start | bytes 3538948
  1522.3 294.1 %copy-start.2 = (f32[512,1024]{1,0:T(8,128)}, f32[512,1024]{1,0:T(8,128)S(1)}, u32[]{:S(2)}) copy-start(f32[512,1024]{1,0:T(8,128)S(1)} %fusion.104) | copy-start | bytes 6291460
  1522.4 294.1 %copy-start.59 = (f32[1024]{0:T(1024)S(1)}, f32[1024]{0:T(1024)}, u32[]{:S(2)}) copy-start(f32[1024]{0:T(1024)} %param.34) | copy-start | bytes 12292
  1524.7 295.4 %copy-start.77 = (f32[768]{0:T(1024)S(1)}, f32[768]{0:T(1024)}, u32[]{:S(2)}) copy-start(f32[768]{0:T(1024)} %param.35) | copy-start | bytes 9220
  1816.4 3.7 copy-start.43
  1816.4 3.7 copy-start.71
  1820.1 4.1 copy-start.57
  1824.2 3.8 copy-start.66
  1824.2 3.9 copy-start.72
  1832.1 3.9 copy-start.44
  1832.1 3.9 copy-start.73
  1840.0 3.9 copy-start.74
  1847.1 8.4 copy-start.51
  1855.4 6.0 copy-start.63
  1855.4 6.0 copy-start.46
  1855.5 6.0 copy-start.75
  1871.3 6.2 copy-start.61
  1871.3 6.2 copy-start.47
  1871.3 6.2 copy-start.76
  1878.8 259.0 %copy-start.55 = (f32[768]{0:T(1024)S(1)}, f32[768]{0:T(1024)}, u32[]{:S(2)}) copy-start(f32[768]{0:T(1024)} %param.31) | copy-start | bytes 9220
  1878.8 259.0 %copy-start.56 = (f32[768]{0:T(1024)S(1)}, f32[768]{0:T(1024)}, u32[]{:S(2)}) copy-start(f32[768]{0:T(1024)} %param.30) | copy-start | bytes 9220
  2441.4 7.9 copy-start.27
  2441.4 23.3 slice-start
  2449.3 21.0 copy-start.7
  2449.3 15.3 slice-start.1
  2464.6 4.6 copy-start.25
  2464.6 4.5 copy-start.26
  2464.6 4.5 copy-start.65
  2504.6 4.7 copy-start.48
  2510.8 7.7 copy-start.52
  2510.8 16.7 slice-start.5
  2510.8 16.7 slice-start.6
  2518.5 9.0 slice-start.7
  2527.5 6.9 copy-start.38
  2544.7 6.8 copy-start.50
  2544.7 16.0 slice-start.2
  2544.7 16.0 slice-start.3
  2551.5 23.7 copy-start.29
  2551.5 9.2 slice-start.4
  2560.7 7.1 copy-start.36
  (47 other events, 82.6 us)
Sparse Core Ops, SparseCore 0:
  9.7 302.0 all-gather.24
  313.5 298.6 all-gather.22
  613.9 298.6 all-gather.18
  914.2 298.6 all-gather.26
  1214.5 301.3 all-gather.20
  1517.4 298.9 all-gather.14
  1818.1 311.9 all-gather.28
  2131.8 309.5 all-gather.16
where the time goes:
time: 2680 us; the launch traced here: 2670 us
  waiting for transfers between devices  2320 us (87%)
  matrix products  190 us (7%)
  blocking collectives  66.1 us (2%)
  local copies, waits for them, and re-layouts  55.3 us (2%)
  other arithmetic  30.1 us (1%)
    all_gather x1, waiting for transfers between devices, shards(): lax.all_gather(shared_a, ('dp', 'fsdp'), axis=0, tiled=True)  300 us
    all_gather x1, waiting for transfers between devices, shards(): lax.all_gather(w_out, ('dp', 'fsdp'), axis=0, tiled=True)  298 us
    all_gather x1, waiting for transfers between devices, shards(): lax.all_gather(w_value, ('dp', 'fsdp'), axis=0, tiled=True)  297 us
    all_gather x1, waiting for transfers between devices, shards(): lax.all_gather(w_key, ('dp', 'fsdp'), axis=0, tiled=True)  296 us
    all_gather x1, waiting for transfers between devices, shards(): lax.all_gather(w_query, ('dp', 'fsdp'), axis=0, tiled=True)  293 us
    all_gather x1, waiting for transfers between devices, shards(): lax.all_gather(shared_b, ('dp', 'fsdp'), axis=0, tiled=True)  292 us
    all_gather x1, waiting for transfers between devices, shards(): lax.all_gather(w_down, ('dp', 'fsdp'), axis=0, tiled=True)  285 us
    all_gather x1, waiting for transfers between devices, shards(): lax.all_gather(w_up, ('dp', 'fsdp'), axis=0, tiled=True)  251 us
  transfers between devices with their start and end apart: 8, of which 8 were waited for; matrix products, arithmetic and copies ran while one was open for 4% of the time, Pallas kernels for 0%

commit v1 on v0

v1 whole, which is shorter than its diff:
```python
import jax
import jax.numpy as jnp
from jax import lax
from jax.experimental import pallas as pl
from jax.experimental.pallas import tpu as pltpu
from jax.sharding import PartitionSpec as P

MESH = pl.DeviceIdType.MESH
BF = jnp.bfloat16
F32 = jnp.float32


def place():
    dp = lax.axis_index("dp")
    fs = lax.axis_index("fsdp")
    return dict(x=fs % 4, y=(dp // 2) * 2 + (fs // 4) % 2, z=fs // 8, c=dp % 2)


def device(at):
    return ((at["y"] // 2) * 2 + at["c"], at["z"] * 8 + (at["y"] % 2) * 4 + at["x"])


def moved(at, axis, delta):
    size = 2 if axis == "c" else 4
    return {**at, axis: (at[axis] + delta + size) % size}


ORDERS = (("x", "y", "z"), ("y", "z", "x"), ("z", "x", "y"))
PEERS = 13


def peers(at):
    found = []
    for dx in range(4):
        for dy in range(2):
            if dx or dy:
                found.append({**at, "x": (at["x"] + dx) % 4, "y": (at["y"] // 2) * 2 + (at["y"] + dy) % 2})
    for dy in range(2):
        found.append({**at, "y": (1 - at["y"] // 2) * 2 + dy})
    for delta in range(1, 4):
        found.append(moved(at, "z", delta))
    found.append(moved(at, "c", 1))
    return found


def enter_signal(at):
    for peer in peers(at):
        pl.semaphore_signal(pltpu.get_barrier_semaphore(), inc=1, device_id=device(peer), device_id_type=MESH)


def region(buf, kind, rot, done, at, low, high):
    every = slice(None)
    x, y, z, c = at["x"], at["y"], at["z"], at["c"]
    yh = every if "y" in done else y // 2
    yl = every if "y" in done else y % 2
    zs = every if "z" in done else z
    if kind == "panel":
        col = every if "x" in done else pl.ds(pl.multiple_of(x * 128, 128), 128)
        return buf.at[low:high, yl, yh, c, zs, rot, :, col]
    col = every if "x" in done else pl.ds(pl.multiple_of((x % 2) * 384, 128), 384)
    half = every if "x" in done else x // 2
    if kind == "down":
        return buf.at[yh, c, zs, yl, half, rot, :, col]
    return buf.at[yh, c, zs, yl, half, :, col]


class Moves:
    def __init__(self, at, bufs, send, recv):
        self.at, self.bufs, self.send, self.recv = at, bufs, send, recv
        self.slots = {}

    def slot(self, key):
        return self.slots.setdefault(key, len(self.slots))

    def copies(self, group, phase):
        kind, low, high = group
        buf = self.bufs[kind]
        for rot in (1,) if kind == "up_b" else range(3):
            order = ORDERS[rot]
            axis, done = order[phase], order[:phase]
            for delta in (1, 3, 2):
                k = self.slot((group, phase, rot, delta))
                yield (
                    region(buf, kind, rot, done, self.at, low, high),
                    moved(self.at, axis, delta),
                    region(buf, kind, rot, done, moved(self.at, axis, -delta), low, high),
                    k,
                )

    def sibling(self, group):
        kind, low, high = group
        buf = self.bufs[kind]
        k = self.slot((group, "c"))
        for here in (self.at,):
            other = moved(here, "c", 1)
            if kind == "panel":
                mine, theirs = buf.at[low:high, :, :, here["c"]], buf.at[low:high, :, :, other["c"]]
            else:
                mine, theirs = buf.at[:, here["c"]], buf.at[:, other["c"]]
            yield mine, other, theirs, k

    def make(self, what):
        mine, target, theirs, k = what
        return pltpu.make_async_remote_copy(
            src_ref=mine,
            dst_ref=mine,
            send_sem=self.send.at[k],
            recv_sem=self.recv.at[k],
            device_id=device(target),
            device_id_type=MESH,
        )

    def arrival(self, what):
        mine, target, theirs, k = what
        return pltpu.make_async_remote_copy(
            src_ref=theirs,
            dst_ref=theirs,
            send_sem=self.send.at[k],
            recv_sem=self.recv.at[k],
            device_id=device(target),
            device_id_type=MESH,
        )

    def listed(self, group, phase):
        return self.sibling(group) if phase == 3 else self.copies(group, phase)

    def start(self, group, phase):
        for what in self.listed(group, phase):
            self.make(what).start()

    def wait(self, group, phase):
        for what in self.listed(group, phase):
            self.arrival(what).wait_recv()

    def sent(self, group, phase):
        for what in self.listed(group, phase):
            self.make(what).wait_send()


def stage_zero(at, shards, packed, landed, half_d, half_b, rows, bufs, send, recv):
    w_query, w_key, w_value, w_out, w_up, w_down, shared_a, shared_b = shards
    kvqo = (w_key, w_value, w_query, w_out)
    x, y, z, c = at["x"], at["y"], at["z"], at["c"]
    mine = (y % 2) * 4 + x

    def pick(ch, yl, dx):
        col = yl * 512 + dx * 128
        if ch == 0:
            return shared_a[:, col : col + 128]
        if ch < 4:
            whole = (ch - 1) * 1024 + col
            return kvqo[whole // 768][:, whole % 768 : whole % 768 + 128]
        whole = (ch - 4) * 1024 + col
        return w_up[:, whole : whole + 128]

    for yl in range(2):
        for dx in range(4):
            for ch in range(7):
                packed[yl * 4 + dx, :, ch * 128 : ch * 128 + 128] = pick(ch, yl, dx)
    landed[pl.ds(mine, 1)] = packed[pl.ds(mine, 1)]
    pl.semaphore_wait(pltpu.get_barrier_semaphore(), PEERS)
    sends, arrivals = [], []
    for step in range(1, 8):
        dx, dy = step % 4, step // 4
        to = {**at, "x": (x + dx) % 4, "y": (y // 2) * 2 + (y + dy) % 2}
        fro = {**at, "x": (x - dx + 4) % 4, "y": (y // 2) * 2 + (y + dy) % 2}
        to_i, fro_i = (to["y"] % 2) * 4 + to["x"], (fro["y"] % 2) * 4 + fro["x"]
        sends.append(pltpu.make_async_remote_copy(
            src_ref=packed.at[to_i], dst_ref=landed.at[mine], send_sem=send.at[step], recv_sem=recv.at[step],
            device_id=device(to), device_id_type=MESH))
        arrivals.append(pltpu.make_async_remote_copy(
            src_ref=packed.at[to_i], dst_ref=landed.at[fro_i], send_sem=send.at[step], recv_sem=recv.at[step],
            device_id=device(to), device_id_type=MESH))
    other = {**at, "x": x + 1 - 2 * (x % 2)}
    col = pl.ds(pl.multiple_of((1 - x % 2) * 384, 128), 384)
    for k, (src, dst) in enumerate(((w_down.at[:, col], half_d), (shared_b.at[:, col], half_b))):
        sends.append(pltpu.make_async_remote_copy(
            src_ref=src, dst_ref=dst, send_sem=send.at[8 + k], recv_sem=recv.at[8 + k],
            device_id=device(other), device_id_type=MESH))
        arrivals.append(sends[-1])
    for copy in sends:
        copy.start()
    for copy in arrivals:
        copy.wait_recv()
    for i in range(8):
        rows[6 * i : 6 * i + 6, :] = landed[i].astype(F32)
    yh, yl = y // 2, y % 2
    block = rows[...].astype(BF).reshape(3, 16, 896)
    own = pl.ds(pl.multiple_of(x * 128, 128), 128)
    for ch in range(7):
        bufs["panel"][ch, yl, yh, c, z, :, :, own] = block[:, :, ch * 128 : ch * 128 + 128]
    keep = pl.ds(pl.multiple_of((x % 2) * 384, 128), 384)
    even = x % 2 == 0
    for src, got, kind in ((w_down, half_d, "down"), (shared_b, half_b, "up_b")):
        a, b = src[:, keep].astype(F32), got[...].astype(F32)
        pair = jnp.concatenate([jnp.where(even, a, b), jnp.where(even, b, a)], axis=0).astype(BF)
        if kind == "down":
            bufs[kind][yh, c, z, yl, x // 2, :, :, keep] = pair.reshape(3, 16, 384)
        else:
            bufs[kind][yh, c, z, yl, x // 2, :, keep] = pair
    for copy in sends:
        copy.wait_send()


PANEL = (7, 2, 2, 2, 4, 3, 16, 512)
DOWN = (2, 2, 4, 2, 2, 3, 16, 768)
UP_B = (2, 2, 4, 2, 2, 16, 768)


LOG2E = 1.4426950408889634
SCALE_Q = 0.125 * LOG2E
NT = (((1,), (1,)), ((), ()))
TN = (((0,), (0,)), ((), ()))
NN = (((1,), (0,)), ((), ()))
FAR = -1e30


def dot(left, right, dims=NN):
    return lax.dot_general(left, right, dims, preferred_element_type=F32)


def span(start, size):
    return pl.ds(pl.multiple_of(start, size), size)


def panel_of(s, ch, half, cols=slice(None)):
    part = s["panel"][ch, half, :, :, :, :, :, cols]
    return part.reshape(768, part.shape[-1])


def first_half(width=128):
    return lax.broadcasted_iota(jnp.int32, (1, width), 1) < 64


def rank_down(s):
    def half(i, _):
        hb, m = i // 2, i % 2
        rows, cols = span(m * 512, 512), span(hb * 512, 512)
        lat = dot(s["x"][m], panel_of(s, 0, hb))
        s["lat"][rows, cols] = lat.astype(BF)
        s["e"][2 * m + hb] = (lat * s["scale_dq"][:, cols]).astype(BF)
        s["e"][4 + 2 * m + hb] = (lat * s["scale_dv"][:, cols]).astype(BF)
        return 0

    lax.fori_loop(0, 4, half, 0)


def project_keys(s):
    x = s["x"][...].reshape(1024, 768)
    s["qkv"][:, 0:512] = dot(x, panel_of(s, 1, 0)).astype(BF)
    s["qkv"][:, 512:768] = dot(x, panel_of(s, 1, 1, slice(0, 256))).astype(BF)


def project_vera(s, slot, base, tile, ch, half, off, scale, kept, factor):
    cols = slice(tile * 256, tile * 256 + 256)
    up = s["up_b"][:, :, :, :, :, :, cols].reshape(1024, 256)

    def micro(m, _):
        rows = span(m * 512, 512)
        t = dot(s["e"][slot + 2 * m], up[:512]) + dot(s["e"][slot + 2 * m + 1], up[512:])
        s[kept][rows, cols] = t.astype(BF)
        full = dot(s["x"][m], panel_of(s, ch, half, slice(off, off + 256))) + s[scale][:, cols] * t
        s["qkv"][rows, base + tile * 256 : base + tile * 256 + 256] = (full * factor if factor else full).astype(BF)
        return 0

    lax.fori_loop(0, 2, micro, 0)


def project_values(s):
    for tile, (ch, half, off) in enumerate(((1, 1, 256), (2, 0, 0), (2, 0, 256))):
        project_vera(s, 4, 768, tile, ch, half, off, "scale_bv", "vt", None)


def project_queries(s, tiles):
    for tile, (ch, half, off) in enumerate(((2, 1, 0), (2, 1, 256), (3, 0, 0))):
        if tile in tiles:
            project_vera(s, 0, 1536, tile, ch, half, off, "scale_bq", "qt", SCALE_Q)


def masks(s, m):
    pos = lax.broadcasted_iota(jnp.int32, (512, 128), 0)
    lane = lax.broadcasted_iota(jnp.int32, (512, 128), 1) % 64
    end = jnp.int32(0)
    pair = jnp.zeros((512, 128), jnp.int32)
    for p in range(4):
        end = end + s["parts"][m, 0, 2 * p] + s["parts"][m, 0, 2 * p + 1]
        pair = pair + (pos >= end).astype(jnp.int32)
    own = lane == pair
    s["mq"][...] = jnp.where(own, 1.0, 0.0).astype(BF)
    s["mk"][...] = jnp.where(own | (lane >= 8), 0.0, FAR).astype(BF)


def scores(s, buf, rows, p, h):
    mine = first_half() if h == 0 else ~first_half()
    k = jnp.where(mine, s["qkv"][rows, span(p * 128, 128)], s["mk"][...])
    q = jnp.where(mine, s["qkv"][rows, span(1536 + p * 128, 128)], s["mq"][...])
    buf[:, :512] = dot(q, k, NT)


def mix(s, buf, rows, p, h, slot):
    mine = first_half() if h == 0 else ~first_half()
    v = s["qkv"][rows, span(768 + p * 128, 128)]
    sc = buf[:, :512]
    e = jnp.exp2(sc - jnp.max(sc, axis=1, keepdims=True)).astype(BF)
    s["e"][slot] = e
    return dot(e, jnp.where(mine, v, jnp.ones_like(v)))


def attend(s):
    def micro(m, _):
        masks(s, m)
        rows = span(m * 512, 512)
        scores(s, s["f_a"], rows, 0, 0)

        def pair(p, _):
            cols = span(p * 128, 128)
            scores(s, s["g_one"].at[0:512, :], rows, p, 1)
            o0 = mix(s, s["f_a"], rows, p, 0, m * 12 + 2 * p)
            scores(s, s["f_a"], rows, jnp.minimum(p + 1, 5), 0)
            o1 = mix(s, s["g_one"].at[0:512, :], rows, p, 1, m * 12 + 2 * p + 1)
            total = pltpu.roll(jnp.where(first_half(), o1, o0), 64, 1)
            inverse = 1.0 / total
            s["inv"][rows, cols] = inverse.astype(BF)
            s["att"][rows, cols] = (jnp.where(first_half(), o0, o1) * inverse).astype(BF)
            return 0

        lax.fori_loop(0, 6, pair, 0)
        return 0

    lax.fori_loop(0, 2, micro, 0)


def mean(v):
    return jnp.mean(v, axis=1, keepdims=True)


def norm(v):
    centred = v - mean(v)
    r = lax.rsqrt(mean(centred * centred) + 1e-05)
    return centred * r, r


def norm_back(hat, r, g):
    return r * (g - mean(g) - hat * mean(g * hat))


def by_rows(fn, size=128):
    lax.fori_loop(0, 512 // size, lambda i, _: (fn(span(i * size, size)), 0)[1], 0)


def middle(s, m):
    rows = span(m * 512, 512)
    hat, hid, slope = s["f_a"], s["hid"], s["slope"]
    other, low, inv = s["g_one"].at[rows, :], s["ga"].at[rows, :], s["inv"].at[rows, :]
    x, cot = s["x"].at[m], s["cot"].at[m]
    att = s["att"][rows, :]
    hat[:, 0:256] = dot(att, panel_of(s, 3, 0, slice(256, 512)))
    hat[:, 256:768] = dot(att, panel_of(s, 3, 1))

    def norm_one(r):
        n, r1 = norm(x[r, :].astype(F32) + hat[r, :])
        hat[r, :] = n
        low[r, :] = (n * s["gain_one"][...] + s["shift_one"][...]).astype(BF)
        s["r1"][r, :] = r1

    by_rows(norm_one)

    def up(t, _):
        u = dot(low[...], panel_of(s, 4 + t // 2, t % 2))
        cdf = 0.5 * (1.0 + lax.erf(u * 0.7071067811865476))
        cols = span(t * 512, 512)
        hid[:, cols] = (u * cdf).astype(BF)
        slope[:, cols] = (cdf + u * (jnp.exp(-0.5 * u * u) * 0.3989422804014327)).astype(BF)
        return 0

    lax.fori_loop(0, 6, up, 0)
    other[...] = dot(hid[...], s["down"][...].reshape(3072, 768))

    def norm_two(r):
        n2, r2 = norm(hat[r, :] * s["gain_one"][...] + s["shift_one"][...] + other[r, :])
        x[r, :] = (n2 * s["gain_two"][...] + s["shift_two"][...]).astype(BF)
        g = norm_back(n2, r2, cot[r, :].astype(F32) * s["gain_two"][...])
        other[r, :] = g
        low[r, :] = g.astype(BF)

    by_rows(norm_two)

    def back(t, _):
        w = s["down"][t // 2, t % 2].reshape(768, 768)
        cols = span(t * 768, 768)
        hid[:, cols] = (dot(low[...], w, NT) * slope[:, cols].astype(F32)).astype(BF)
        return 0

    lax.fori_loop(0, 4, back, 0)

    def first(t, _):
        other[...] += dot(hid[:, span(t * 512, 512)], panel_of(s, 4 + t // 2, t % 2), NT)
        return 0

    lax.fori_loop(0, 6, first, 0)

    def norm_one_back(r):
        g = norm_back(hat[r, :], s["r1"][r, :], other[r, :] * s["gain_one"][...])
        other[r, :] = g
        low[r, :] = g.astype(BF)

    by_rows(norm_one_back)
    hat[...] = dot(low[:, :256], panel_of(s, 3, 0, slice(256, 512)), NT) + dot(low[:, 256:], panel_of(s, 3, 1), NT)

    def scale_att(r):
        low[r, :] = (hat[r, :] * inv[r, :].astype(F32)).astype(BF)

    by_rows(scale_att)


def attend_back(s):
    def micro(m, _):
        rows = span(m * 512, 512)

        def pair(p, _):
            kc, vc, qc = span(p * 128, 128), span(768 + p * 128, 128), span(1536 + p * 128, 128)
            k, v, q = s["qkv"][rows, kc], s["qkv"][rows, vc], s["qkv"][rows, qc]
            ga = s["ga"][rows, kc]
            prod = ga.astype(F32) * s["att"][rows, kc].astype(F32)
            gq = gk = gv = None
            lanes = lax.broadcasted_iota(jnp.int32, (1, 128), 1)
            for h in range(2):
                mine = first_half() if h == 0 else ~first_half()
                delta = -jnp.sum(jnp.where(mine, prod, 0.0), axis=1, keepdims=True)
                high = delta.astype(BF)
                rest = (delta - high.astype(F32)).astype(BF)
                zero = jnp.zeros_like(ga)
                gah = jnp.where(mine, ga, zero)
                aug = jnp.where(mine, ga, jnp.where(lanes % 64 == 0, high, jnp.where(lanes % 64 == 1, rest, zero)))
                gp = dot(aug, jnp.where(mine, v, jnp.ones_like(v)), NT)
                e = s["e"][m * 12 + 2 * p + h]
                gs = (e.astype(F32) * gp).astype(BF)
                gvh = dot(e, gah, TN)
                gqh = dot(gs, jnp.where(mine, k, zero))
                gkh = dot(gs, jnp.where(mine, q, zero), TN)
                gq, gk, gv = (gqh, gkh, gvh) if h == 0 else (gq + gqh, gk + gkh, gv + gvh)
            s["qkv"][rows, qc] = (gq * 0.125).astype(BF)
            s["qkv"][rows, kc] = (gk * (1.0 / LOG2E)).astype(BF)
            s["qkv"][rows, vc] = gv.astype(BF)
            return 0

        lax.fori_loop(0, 6, pair, 0)
        return 0

    lax.fori_loop(0, 2, micro, 0)


def vera_back(s):
    for base, kept, scale, row, keep in ((1536, "qt", "scale_bq", 1, "att"), (768, "vt", "scale_bv", 3, "ga")):

        def block(i, total):
            rows = span(i * 128, 128)
            g = s["qkv"][rows, base : base + 768].astype(F32)
            s[keep][rows, :] = (g * s[scale][...]).astype(BF)
            return total + jnp.sum(g * s[kept][rows, :].astype(F32), axis=0, keepdims=True)

        s["red"][row : row + 1, 0:768] = lax.fori_loop(0, 8, block, jnp.zeros((1, 768), F32))

    def half(hb, _):
        cols = span(hb * 512, 512)
        w = s["up_b"][hb].reshape(512, 768)
        for m in range(2):
            rows = slice(m * 512, m * 512 + 512)
            gqu, gvu = dot(s["att"][rows, :], w, NT), dot(s["ga"][rows, :], w, NT)
            lat = s["lat"][rows, cols].astype(F32)
            for row, val in ((0, gqu), (2, gvu)):
                part = jnp.sum(val * lat, axis=0, keepdims=True)
                if m:
                    part = part + s["red"][row : row + 1, cols]
                s["red"][row : row + 1, cols] = part
            s["e"][2 * m + hb] = (gqu * s["scale_dq"][:, cols] + gvu * s["scale_dv"][:, cols]).astype(BF)
        return 0

    lax.fori_loop(0, 2, half, 0)


def token_grads(s, m):
    rows = slice(m * 512, m * 512 + 512)
    total = s["f_a"]

    def projections(i, _):
        total[...] += dot(s["qkv"][rows, span(i * 512, 512)], panel_of(s, 1 + i // 2, i % 2), NT)
        return 0

    def latents(hb, _):
        total[...] += dot(s["e"][2 * m + hb], panel_of(s, 0, hb), NT)
        return 0

    total[...] = s["g_one"][rows, :] + dot(s["qkv"][rows, 2048:2304], panel_of(s, 3, 0, slice(0, 256)), NT)
    lax.fori_loop(0, 4, projections, 0)
    lax.fori_loop(0, 2, latents, 0)
    s["cot"][m] = total[...].astype(BF)


LAYER_SCRATCH = dict(
    panel=(PANEL, BF),
    down=(DOWN, BF),
    up_b=(UP_B, BF),
    x=((2, 512, 768), BF),
    cot=((2, 512, 768), BF),
    lat=((1024, 1024), BF),
    qt=((1024, 768), BF),
    vt=((1024, 768), BF),
    qkv=((1024, 2304), BF),
    e=((24, 512, 512), BF),
    att=((1024, 768), BF),
    inv=((1024, 768), BF),
    ga=((1024, 768), BF),
    g_one=((1024, 768), F32),
    f_a=((512, 768), F32),
    hid=((512, 3072), BF),
    slope=((512, 3072), BF),
    mq=((512, 128), BF),
    mk=((512, 128), BF),
    r1=((512, 1), F32),
    red=((4, 1024), F32),
)


VECTORS = ("gain_one", "shift_one", "gain_two", "shift_two", "scale_dq", "scale_bq", "scale_dv", "scale_bv")
SHARDS = ("w_query", "w_key", "w_value", "w_out", "w_up", "w_down", "shared_a", "shared_b")
SHARD_SHAPES = ((6, 768),) * 4 + ((6, 3072), (24, 768), (6, 1024), (8, 768))
GROUP_A, GROUP_1, GROUP_2, GROUP_3 = (("panel", i, i + 1) for i in range(4))
GROUP_UP, GROUP_DOWN, GROUP_B = ("panel", 4, 7), ("down", 0, 0), ("up_b", 0, 0)
EARLY, LATE = (("panel", 0, 4), GROUP_B), (GROUP_UP, GROUP_DOWN)


def reduce_start(at, axis, first, s, send, recv):
    size = 2 if axis == "c" else 4
    here = at[axis]
    s["sums"][pl.ds(first + here, 1)] = s["red"][...][None]
    sends, arrivals = [], []
    for i, delta in enumerate((1, 3, 2) if size == 4 else (1,)):
        to, fro = moved(at, axis, delta), moved(at, axis, -delta)
        for found, slot in ((sends, here), (arrivals, fro[axis])):
            found.append(pltpu.make_async_remote_copy(
                src_ref=s["sums"].at[first + slot], dst_ref=s["sums"].at[first + slot],
                send_sem=send.at[first + i], recv_sem=recv.at[first + i],
                device_id=device(to), device_id_type=MESH))
    for copy in sends:
        copy.start()
    return sends, arrivals, first, size


def reduce_end(state, s):
    sends, arrivals, first, size = state
    for copy in arrivals:
        copy.wait_recv()
    for copy in sends:
        copy.wait_send()
    total = s["sums"][first] + s["sums"][first + 1]
    if size == 4:
        total = total + (s["sums"][first + 2] + s["sums"][first + 3])
    s["red"][...] = total


EXTRA = dict(
    packed=((8, 6, 896), BF),
    landed=((8, 6, 896), BF),
    half_d=((24, 384), BF),
    half_b=((8, 384), BF),
    rows=((48, 896), F32),
    sums=((14, 4, 1024), F32),
)


def whole(*refs):
    names = ("tokens", "parts_in", "cotangent") + tuple("in_" + n for n in SHARDS) + tuple("in_" + n for n in VECTORS)
    names += ("out", "grad_tokens", "grad_red")
    scratch = tuple(LAYER_SCRATCH) + tuple(EXTRA) + SHARDS + VECTORS
    names += scratch + ("parts", "loads", "send_0", "recv_0", "send", "recv", "send_r", "recv_r")
    s = dict(zip(names, refs, strict=True))
    at = place()
    loads = []
    pairs = [(s["in_" + n], s[n]) for n in SHARDS] + [(s["in_" + n], s[n].at[0]) for n in VECTORS]
    pairs += [(s["parts_in"], s["parts"]), (s["tokens"], s["x"]), (s["cotangent"], s["cot"])]
    for i, (src, dst) in enumerate(pairs):
        loads.append(pltpu.make_async_copy(src, dst, s["loads"].at[i]))
        loads[-1].start()
    enter_signal(at)
    for copy in loads[:8]:
        copy.wait()
    bufs = {k: s[k] for k in ("panel", "down", "up_b")}
    stage_zero(at, [s[n] for n in SHARDS], s["packed"], s["landed"], s["half_d"], s["half_b"], s["rows"], bufs, s["send_0"], s["recv_0"])
    moves = Moves(at, bufs, s["send"], s["recv"])
    begun = []

    def start(group, phase):
        moves.start(group, phase)
        begun.append((group, phase))

    for group in EARLY + LATE:
        start(group, 0)
    for group in EARLY + LATE:
        moves.wait(group, 0)
    for group in EARLY + LATE:
        start(group, 1)
    for group in EARLY:
        moves.wait(group, 1)
    order = (GROUP_A, GROUP_1, GROUP_2, GROUP_B, GROUP_3)
    for group in order:
        start(group, 2)
    for group in LATE:
        moves.wait(group, 1)
    for group in LATE:
        start(group, 2)

    def pass_on(group):
        moves.wait(group, 2)
        start(group, 3)

    pass_on(GROUP_A)
    pass_on(GROUP_1)
    for copy in loads[8:]:
        copy.wait()
    moves.wait(GROUP_A, 3)
    rank_down(s)
    pass_on(GROUP_2)
    moves.wait(GROUP_1, 3)
    project_keys(s)
    pass_on(GROUP_B)
    pass_on(GROUP_3)
    moves.wait(GROUP_2, 3)
    moves.wait(GROUP_B, 3)
    project_values(s)
    project_queries(s, (0, 1))
    moves.wait(GROUP_3, 3)
    project_queries(s, (2,))
    attend(s)
    pass_on(GROUP_UP)
    pass_on(GROUP_DOWN)
    moves.wait(GROUP_UP, 3)
    moves.wait(GROUP_DOWN, 3)
    lax.fori_loop(0, 2, lambda m, _: (middle(s, m), 0)[1], 0)
    result = pltpu.make_async_copy(s["x"], s["out"], s["loads"].at[0])
    result.start()
    for group, phase in begun:
        moves.sent(group, phase)
    attend_back(s)
    vera_back(s)
    for row in (1, 3):
        s["red"][row : row + 1, 768:1024] = jnp.zeros((1, 256), F32)
    state = reduce_start(at, "c", 0, s, s["send_r"], s["recv_r"])
    token_grads(s, 0)
    reduce_end(state, s)
    state = reduce_start(at, "x", 2, s, s["send_r"], s["recv_r"])
    token_grads(s, 1)
    grads = pltpu.make_async_copy(s["cot"], s["grad_tokens"], s["loads"].at[1])
    grads.start()
    reduce_end(state, s)
    for axis, first in (("y", 6), ("z", 10)):
        reduce_end(reduce_start(at, axis, first, s, s["send_r"], s["recv_r"]), s)
    last = pltpu.make_async_copy(s["red"], s["grad_red"], s["loads"].at[2])
    last.start()
    assert len(moves.slots) == 124
    for copy in (last, result, grads):
        copy.wait()


def shards(tokens, parts, cotangent, *rest):
    anywhere = pl.BlockSpec(memory_space=pl.ANY)
    scratch = [pltpu.VMEM(shape, kind) for shape, kind in (*LAYER_SCRATCH.values(), *EXTRA.values())]
    scratch += [pltpu.VMEM(shape, BF) for shape in SHARD_SHAPES]
    scratch += [pltpu.VMEM((1, v.shape[0]), F32) for v in rest[8:]]
    scratch += [pltpu.SMEM((2, 1, 8), jnp.int32)]
    scratch += [pltpu.SemaphoreType.DMA((n,)) for n in (19, 10, 10, 124, 124, 14, 14)]
    out, grad, red = pl.pallas_call(
        whole,
        out_shape=[
            jax.ShapeDtypeStruct((2, 512, 768), BF),
            jax.ShapeDtypeStruct((2, 512, 768), BF),
            jax.ShapeDtypeStruct((4, 1024), F32),
        ],
        in_specs=[anywhere] * 19,
        out_specs=[anywhere] * 3,
        scratch_shapes=scratch,
        compiler_params=pltpu.CompilerParams(collective_id=0, has_side_effects=True, vmem_limit_bytes=63 << 20),
    )(tokens, parts, cotangent, *rest)
    return out, grad, red[0], red[1, :768], red[2], red[3, :768]


def solution(mesh):
    rows, split, same = P(None, ("dp", "fsdp"), None), P(("dp", "fsdp"), None), P()
    return jax.shard_map(
        shards,
        mesh=mesh,
        in_specs=(rows,) * 3 + (split,) * 8 + (same,) * 8,
        out_specs=(rows, rows, same, same, same, same),
        check_vma=False,
    )
```

time: 2680 us -> 166 us (0.06)
  waiting for transfers between devices: 2320 us -> 0 us
  matrix products: 190 us -> 0 us
  Pallas kernels: 0 us -> 158 us
  blocking collectives: 66.1 us -> 0 us
  local copies, waits for them, and re-layouts: 55.3 us -> 6.71 us
  other arithmetic: 30.1 us -> 0 us
    all_gather x8 -> x0, waiting for transfers between devices: 2310 us -> none  [the longest x1 300 us: shards(): lax.all_gather(shared_a, ('dp', 'fsdp'), axis=0, tiled=True)]
    dot_general x44 -> x0, matrix products: 174 us -> none  [the longest x18 72.1 us: product(): return jnp.dot(left, right, preferred_element_type=jnp.float32)]
    pallas_call x0 -> x1, Pallas kernels: none -> 158 us  [shards(): pl.pallas_call(whole, out_shape=[jax.ShapeDtypeStruct((2, 512, 768), BF),...]
    psum x1 -> x0, blocking collectives: 66.1 us -> none  [shards(): lax.psum((running[0], running[1], running[2], running[3]), ('dp', 'fsdp'))]
    unnamed x180 -> x4, local copies, waits for them, and re-layouts: 38.7 us -> 3.92 us
  transfers between devices with their start and end apart: 8 -> 0, of which waited for: 8 -> 0; matrix products, arithmetic and copies ran while one was open for 4% -> 0% of each run, Pallas kernels for 0% -> 0%
where the time goes in v1:
time: 166 us; the launch traced here: 165 us
  Pallas kernels  158 us (95%)
  local copies, waits for them, and re-layouts  6.71 us (4%)
    pallas_call x1, Pallas kernels, shards(): pl.pallas_call(whole, out_shape=[jax.ShapeDtypeStruct((2, 512, 768), BF),...  158 us
    unnamed x4, local copies, waits for them, and re-layouts  3.92 us

profile of v1, /device:TPU:1, one launch (start us, length us, event | category | flops | bytes accessed | tf_op | source)
XLA Modules:
  0.0 165.4 jit_solution(15066415914314391979)
XLA Ops:
  0.6 158.0 %shard_map.226 = (bf16[2,512,768]{2,1,0:T(8,128)(2,1)}, bf16[2,512,768]{2,1,0:T(8,128)(2,1)}, f32[4,1024]{1,0:T(4,128)}) custom-call(bf16[2,512,768]{2,1,0:T(8,128)(2,1)} %refs_0_.1, s32[2,1,8]{2,1,0:T(1,128)} %refs_1_.1, bf16[2,512,768]{2,1,0:T(8,128)(2,1)} %refs_2_.1, bf16[6,768]{1,0:T(8,128)(2,1)} %refs_3_.1, bf16[6,768]{1,0:T(8,128)(2,1)} %refs_4_.1, ...), custom_call_target="tpu_custom_call" | custom-call | tf_op jit(solution)/shard_map/pallas_call | solution.py:672
  158.6 1.4 slice_reduce_fusion
  160.0 1.4 fusion
  161.4 0.0 copy-start
  161.4 2.8 %copy.27 = bf16[2,512,768]{2,1,0:T(8,128)(2,1)} copy(bf16[2,512,768]{2,1,0:T(8,128)(2,1)} %get-tuple-element.22) | data formatting | bytes 3145728
  164.2 0.0 copy-done
  164.2 1.1 copy.28
Async XLA Ops:
  161.4 2.8 %copy-start = (bf16[2,512,768]{2,1,0:T(8,128)(2,1)S(1)}, bf16[2,512,768]{2,1,0:T(8,128)(2,1)}, u32[]{:S(2)}) copy-start(bf16[2,512,768]{2,1,0:T(8,128)(2,1)} %get-tuple-element.23) | copy-start | bytes 4718596
